TPU v7x, 128 devices: a whole 4x4x4 slice. The times are simulated.
128 devices in a mesh: row: 16 (over x, z), col: 8 (over y, core).
Axes of the slice: x: 4, y: 4, z: 4, core: 2. Of those that a mesh axis runs over, the one named last changes fastest.
Arguments:
- excitation: bfloat16 [131072, 128], P(('row', 'col')), may hold values from -6 to 6
- near_list: int32 [1024, 5], P(('row', 'col')), may hold values from 0 to 1023, as said below
- near_blocks: bfloat16 [2, 131072, 640], P(None, ('row', 'col')), may hold values from -0.15625 to 0.15625
- col_factors: bfloat16 [2, 131072, 2048], P(None, ('row', 'col')), may hold values from -0.125 to 0.125
- coupling: bfloat16 [2, 131072, 2048], P(None, ('row', 'col')), may hold values from -0.09375 to 0.09375
- row_factors: bfloat16 [2, 131072, 1024], P(None, ('row', 'col')), may hold values from -0.125 to 0.125
Outputs:
- response: bfloat16 [131072, 128], P(('row', 'col'))
Inputs may be any that keep to these rules, and one draw needn't show every extreme that they name: near_list[i, 0] = i; every entry lies within 8 leaves of i, and leaves at distance exactly 8 on either side occur.
All inputs are finite; a program needn't handle non-finite values.
Results may differ from a plain program's by a relative error of at most 0.008.
Values may be sent and summed in bfloat16 or wider, within the bound.
A program may use at most 128 MiB of HBM per device.

v0:
```python
import jax
import jax.numpy as jnp
from jax import lax
from jax.sharding import PartitionSpec as P

RANK = 128
LEAF = 128
REACH = 8
NEAR = 5


def with_halo(cells, sides, width):
    for axis, dim in sides:
        count = lax.axis_size(axis)
        ends = count - 1
        head = lax.slice_in_dim(cells, 0, width, axis=dim)
        tail = lax.slice_in_dim(cells, cells.shape[dim] - width, cells.shape[dim], axis=dim)
        cells = jnp.concatenate(
            [
                lax.ppermute(tail, axis, [(i, (i + 1) % count) for i in range(ends)]),
                cells,
                lax.ppermute(head, axis, [((i + 1) % count, i) for i in range(ends)]),
            ],
            axis=dim,
        )
    return cells


def signed_swap(width):
    half = width // 2
    source = lax.broadcasted_iota(jnp.int32, (width, width), 0)
    target = lax.broadcasted_iota(jnp.int32, (width, width), 1)
    negative = jnp.where((target < half) & (source == target + half), -1.0, 0.0)
    positive = jnp.where((target >= half) & (source == target - half), 1.0, 0.0)
    return (negative + positive).astype(jnp.bfloat16)


def turn_flat(flat_data):
    rotation = signed_swap(flat_data.shape[1])
    return jnp.dot(flat_data, rotation, preferred_element_type=jnp.float32).astype(jnp.bfloat16)


def multiply_flat(real_part, imag_part, flat_data):
    turned = turn_flat(flat_data)
    summed = jnp.dot(real_part, flat_data, preferred_element_type=jnp.float32)
    return summed + jnp.dot(imag_part, turned, preferred_element_type=jnp.float32)


def project_flat(real_part, imag_part, flat_data):
    turned = turn_flat(flat_data)
    contract_dims = (((0,), (0,)), ((), ()))
    summed = lax.dot_general(
        real_part, flat_data, contract_dims, preferred_element_type=jnp.float32
    )
    return summed + lax.dot_general(
        imag_part, turned, contract_dims, preferred_element_type=jnp.float32
    )


def multiply_split_flat(real_part, imag_part, flat_data):
    upper_part = flat_data.astype(jnp.bfloat16)
    lower_part = (flat_data - upper_part.astype(jnp.float32)).astype(jnp.bfloat16)
    return multiply_flat(real_part, imag_part, upper_part) + multiply_flat(
        real_part, imag_part, lower_part
    )


def on_device(excitation, near_list, near_blocks, col_factors, coupling, row_factors):
    row_total = excitation.shape[0]
    width_cols = excitation.shape[1]
    leaves_here = row_total // LEAF
    row_count = lax.axis_size("row")
    col_count = lax.axis_size("col")
    padded = with_halo(excitation, ((("row", "col"), 0),), REACH * LEAF)
    leaves_pad = leaves_here + 2 * REACH
    table = padded.reshape(leaves_pad, LEAF * width_cols)
    first_leaf = lax.axis_index(("row", "col")) * leaves_here
    local_leaf = near_list - first_leaf + REACH
    slots = lax.broadcasted_iota(jnp.int32, (leaves_here, NEAR, leaves_pad), 2)
    selector = (
        (local_leaf[:, :, None] == slots)
        .astype(jnp.bfloat16)
        .reshape(leaves_here * NEAR, leaves_pad)
    )
    pieces = jnp.dot(selector, table, preferred_element_type=jnp.float32).astype(jnp.bfloat16)
    pieces = pieces.reshape(leaves_here * NEAR * LEAF, width_cols)
    turned = turn_flat(pieces).reshape(leaves_here, NEAR * LEAF, width_cols)
    pieces = pieces.reshape(leaves_here, NEAR * LEAF, width_cols)
    blocks_re = near_blocks[0].reshape(leaves_here, LEAF, NEAR * LEAF)
    blocks_im = near_blocks[1].reshape(leaves_here, LEAF, NEAR * LEAF)
    near_field = jnp.einsum("ilm,imc->ilc", blocks_re, pieces, preferred_element_type=jnp.float32)
    near_field = near_field + jnp.einsum(
        "ilm,imc->ilc", blocks_im, turned, preferred_element_type=jnp.float32
    )
    near_field = near_field.reshape(row_total, width_cols)
    compressed = project_flat(col_factors[0], col_factors[1], excitation)
    shaped = compressed.reshape(row_count, RANK, width_cols)
    arrived = lax.all_to_all(shaped, "row", split_axis=0, concat_axis=0, tiled=True)
    arrived_flat = arrived.reshape(row_count * RANK, width_cols)
    span_width = arrived_flat.shape[1]
    middle = multiply_split_flat(coupling[0], coupling[1], arrived_flat)
    middle = middle.reshape(col_count, RANK, span_width)
    landed = lax.all_to_all(middle, "col", split_axis=0, concat_axis=0, tiled=True)
    far_field = multiply_split_flat(
        row_factors[0], row_factors[1], landed.reshape(col_count * RANK, span_width)
    )
    return (near_field + far_field).astype(jnp.bfloat16)


def solution(mesh):
    return jax.shard_map(
        on_device,
        mesh=mesh,
        in_specs=(
            P(("row", "col"), None),
            P(("row", "col"), None),
            P(None, ("row", "col"), None),
            P(None, ("row", "col"), None),
            P(None, ("row", "col"), None),
            P(None, ("row", "col"), None),
        ),
        out_specs=P(("row", "col"), None),
        check_vma=False,
    )
```

profile of v0, /device:TPU:1, one launch (start us, length us, event | category | flops | bytes accessed | tf_op | source)
XLA Modules:
  0.0 85.9 jit_solution(8925337674729845388)
XLA Ops:
  0.0 3.3 %collective-permute-start.1 = (bf16[1024,128]{1,0:T(8,128)(2,1)}, bf16[1024,128]{1,0:T(8,128)(2,1)S(1)}, u32[]{:S(2)}, u32[]{:S(2)}) collective-permute-start(bf16[1024,128]{1,0:T(8,128)(2,1)} %param.6), channel_id=1, source_target_pairs={{1,0},{2,1},{3,2},{4,3},{5,4},{6,5},{7,6},{8,7},{9,8},{10,9},{11,1... | collective-permute-start | bytes 786440 | tf_op jit(solution)/shard_map/ppermute | solution.py:22
  3.3 3.2 %collective-permute-start = (bf16[1024,128]{1,0:T(8,128)(2,1)}, bf16[1024,128]{1,0:T(8,128)(2,1)S(1)}, u32[]{:S(2)}, u32[]{:S(2)}) collective-permute-start(bf16[1024,128]{1,0:T(8,128)(2,1)} %param.6), channel_id=1, source_target_pairs={{0,1},{1,2},{2,3},{3,4},{4,5},{5,6},{6,7},{7,8},{8,9},{9,10},{10,1... | collective-permute-start | bytes 786440 | tf_op jit(solution)/shard_map/ppermute | solution.py:20
  6.6 3.5 %fusion.10 = f32[2048,128]{1,0:T(8,128)S(1)} fusion(bf16[1024,128]{1,0:T(8,128)(2,1)} %param.6, bf16[2,1024,2048]{2,1,0:T(8,128)(2,1)} %param.9), kind=kOutput, calls=%fused_computation.12 | convolution fusion | flops 536870912 | bytes 5505024 | tf_op jit(solution)/shard_map/dot_general | solution.py:52
  10.1 5.0 %fusion.21 = f32[2048,128]{1,0:T(8,128)} fusion(f32[2048,128]{1,0:T(8,128)S(1)} %fusion.10, bf16[2,1024,2048]{2,1,0:T(8,128)(2,1)} %param.9, bf16[1024,128]{1,0:T(8,128)(2,1)S(1)} %copy-done.2, s32[128]{0:T(128)S(1)} %get-tuple-element.15, s32[128]{0:T(128)S(1)} %get-tuple-element.16, pred[128]{0:T(512)(128)(4,1)S(1)} %get-tuple-element.17, ...), kind=kOutput, calls=%fused_computation.21 | convolution fusion | flops 570949632 | bytes 6554880 | tf_op jit(solution)/shard_map/dot_general | solution.py:55
  15.1 7.6 %all-to-all-start = ((f32[16,128,128]{2,1,0:T(8,128)}), f32[16,128,128]{2,1,0:T(8,128)S(1)}, u32[]{:S(2)}, u32[]{:S(2)}) async-start(f32[16,128,128]{2,1,0:T(8,128)} %bitcast.8), calls=%async_computation | async-start | bytes 2097152 | tf_op jit(solution)/shard_map/all_to_all | solution.py:98
  22.7 3.4 %fusion.103 = (bf16[1,1024,640]{2,1,0:T(8,128)(2,1)}, bf16[1,1024,640]{2,1,0:T(8,128)(2,1)}) fusion(bf16[2,1024,640]{2,1,0:T(8,128)(2,1)} %param.8), kind=kLoop, calls=%fused_computation.89 | loop fusion | bytes 5242880 | tf_op jit(solution)/shard_map/slice | solution.py:90
  27.1 1.7 %reshape_reshape.3 = bf16[8,640,128]{2,1,0:T(8,128)(2,1)} reshape(bf16[40,16384]{1,0:T(8,128)(2,1)S(1)} %convolution_convert_fusion) | data formatting | bytes 2621440 | tf_op jit(solution)/shard_map/reshape;reshape | solution.py:88
  28.8 1.7 %reshape.64 = bf16[5120,128]{1,0:T(8,128)(2,1)} reshape(bf16[40,16384]{1,0:T(8,128)(2,1)S(1)} %convolution_convert_fusion) | data formatting | bytes 2621440 | tf_op jit(solution)/shard_map/reshape | solution.py:86
  30.4 2.2 %fusion.104 = f32[8,128,128]{1,2,0:T(8,128)S(1)} fusion(bf16[8,128,640]{2,1,0:T(8,128)(2,1)} %bitcast.107, bf16[8,640,128]{2,1,0:T(8,128)(2,1)} %reshape_reshape.3), kind=kOutput, calls=%fused_computation.90 | convolution fusion | flops 167772160 | bytes 3145728 | tf_op jit(solution)/shard_map/ilm,imc->ilc/dot_general | solution.py:91
  32.7 5.2 %all-to-all-done = f32[16,128,128]{2,1,0:T(8,128)S(1)} async-done(((f32[16,128,128]{2,1,0:T(8,128)}), f32[16,128,128]{2,1,0:T(8,128)S(1)}, u32[]{:S(2)}, u32[]{:S(2)}) %all-to-all-start) | async-done | bytes 1048608 | tf_op jit(solution)/shard_map/all_to_all | solution.py:98
  38.0 3.9 %fusion.2 = f32[128,1024]{1,0:T(8,128)S(1)} fusion(bf16[2,1024,2048]{2,1,0:T(8,128)(2,1)} %param.10, bf16[2048,128]{1,0:T(8,128)(2,1)S(1)} %get-tuple-element.12, s32[128]{0:T(128)S(1)} %get-tuple-element.15, s32[128]{0:T(128)S(1)} %get-tuple-element.16, pred[128]{0:T(512)(128)(4,1)S(1)} %get-tuple-element.17, pred[128]{0:T(512)(128)(4,1)S(1)} %get-tuple-element.18), kind=kOutput, calls=%fused_computation.4 | convolution fusion | flops 604372992 | bytes 5244160 | tf_op jit(solution)/shard_map/dot_general | solution.py:46
  41.9 4.7 %fusion = f32[128,1024]{1,0:T(8,128)} fusion(bf16[2,1024,2048]{2,1,0:T(8,128)(2,1)} %param.10, bf16[2048,128]{1,0:T(8,128)(2,1)S(1)} %get-tuple-element.11, s32[128]{0:T(128)S(1)} %get-tuple-element.15, s32[128]{0:T(128)S(1)} %get-tuple-element.16, pred[128]{0:T(512)(128)(4,1)S(1)} %get-tuple-element.17, pred[128]{0:T(512)(128)(4,1)S(1)} %get-tuple-element.18), kind=kOutput, calls=%fused_computation.2 | convolution fusion | flops 604372992 | bytes 5244160 | tf_op jit(solution)/shard_map/dot_general | solution.py:46
  46.9 3.8 %fusion.51 = f32[128,1024]{1,0:T(8,128)S(1)} fusion(f32[128,1024]{1,0:T(8,128)S(1)} %fusion.2, bf16[2048,128]{1,0:T(8,128)(2,1)S(1)} %bitcast.114, bf16[2,1024,2048]{2,1,0:T(8,128)(2,1)} %param.10), kind=kOutput, calls=%fused_computation.42 | convolution fusion | flops 537001984 | bytes 5767168 | tf_op jit(solution)/shard_map/dot_general | solution.py:45
  50.7 3.8 %fusion.60 = f32[16,8,8,128]{3,2,1,0:T(8,128)S(1)} fusion(f32[128,1024]{1,0:T(8,128)S(1)} %fusion.51, f32[128,1024]{1,0:T(8,128)S(1)} %copy-done.4, bf16[2048,128]{1,0:T(8,128)(2,1)S(1)} %bitcast.113, bf16[2,1024,2048]{2,1,0:T(8,128)(2,1)} %param.10), kind=kOutput, calls=%fused_computation.45 | convolution fusion | flops 537133056 | bytes 6291456 | tf_op jit(solution)/shard_map/dot_general | solution.py:45
  54.6 0.8 copy.27
  55.4 8.5 %all-to-all-start.1 = ((f32[8,128,128]{1,2,0:T(8,128)}), f32[8,128,128]{1,2,0:T(8,128)}, u32[]{:S(2)}, u32[]{:S(2)}) async-start(f32[8,128,128]{1,2,0:T(8,128)} %bitcast.110), calls=%async_computation.1 | async-start | bytes 1048576 | tf_op jit(solution)/shard_map/all_to_all | solution.py:103
  64.4 0.5 convolution_add_fusion
  65.2 8.4 %all-to-all-done.1 = f32[8,128,128]{1,2,0:T(8,128)} async-done(((f32[8,128,128]{1,2,0:T(8,128)}), f32[8,128,128]{1,2,0:T(8,128)}, u32[]{:S(2)}, u32[]{:S(2)}) %all-to-all-start.1) | async-done | bytes 524320 | tf_op jit(solution)/shard_map/all_to_all | solution.py:103
  73.5 1.2 %copy.19 = f32[8,128,128]{2,1,0:T(8,128)S(1)} copy(f32[8,128,128]{1,2,0:T(8,128)} %all-to-all-done.1) | data formatting | bytes 1048576 | tf_op jit(solution)/shard_map/all_to_all | solution.py:103
  75.0 2.6 %fusion.24 = f32[128,1024]{1,0:T(8,128)S(1)} fusion(bf16[2,1024,1024]{2,1,0:T(8,128)(2,1)} %param.11, bf16[1024,128]{1,0:T(8,128)(2,1)S(1)} %get-tuple-element.7, s32[128]{0:T(128)S(1)} %get-tuple-element.15, s32[128]{0:T(128)S(1)} %get-tuple-element.16, pred[128]{0:T(512)(128)(4,1)S(1)} %get-tuple-element.17, pred[128]{0:T(512)(128)(4,1)S(1)} %get-tuple-element.18), kind=kOutput, calls=%fused_computation.24 | convolution fusion | flops 302252032 | bytes 2884864 | tf_op jit(solution)/shard_map/dot_general | solution.py:46
  77.6 2.6 %fusion.26 = f32[128,1024]{1,0:T(8,128)S(1)} fusion(bf16[2,1024,1024]{2,1,0:T(8,128)(2,1)} %param.11, bf16[1024,128]{1,0:T(8,128)(2,1)S(1)} %get-tuple-element.8, s32[128]{0:T(128)S(1)} %get-tuple-element.15, s32[128]{0:T(128)S(1)} %get-tuple-element.16, pred[128]{0:T(512)(128)(4,1)S(1)} %get-tuple-element.17, pred[128]{0:T(512)(128)(4,1)S(1)} %get-tuple-element.18), kind=kOutput, calls=%fused_computation.26 | convolution fusion | flops 302252032 | bytes 2884864 | tf_op jit(solution)/shard_map/dot_general | solution.py:46
  80.2 2.4 %fusion.48 = f32[128,1024]{1,0:T(8,128)S(1)} fusion(f32[128,1024]{1,0:T(8,128)S(1)} %fusion.24, bf16[1024,128]{1,0:T(8,128)(2,1)S(1)} %bitcast.112, bf16[2,1024,1024]{2,1,0:T(8,128)(2,1)} %param.11), kind=kOutput, calls=%fused_computation.40 | convolution fusion | flops 268566528 | bytes 3407872 | tf_op jit(solution)/shard_map/dot_general | solution.py:45
  82.6 2.5 %fusion.63 = bf16[1024,128]{0,1:T(8,128)(2,1)S(1)} fusion(f32[1024,128]{0,1:T(8,128)S(1)} %copy.22, f32[128,1024]{1,0:T(8,128)S(1)} %fusion.48, f32[128,1024]{1,0:T(8,128)S(1)} %fusion.26, bf16[1024,128]{1,0:T(8,128)(2,1)S(1)} %bitcast.111, bf16[2,1024,1024]{2,1,0:T(8,128)(2,1)} %param.11), kind=kOutput, calls=%fused_computation.46 | convolution fusion | flops 268959744 | bytes 4194304 | tf_op jit(solution)/shard_map/dot_general | solution.py:45
  85.1 0.8 copy.23
  (26 shorter events, 2.3 us)
Async XLA Ops:
  0.0 26.2 %collective-permute-start.1 = (bf16[1024,128]{1,0:T(8,128)(2,1)}, bf16[1024,128]{1,0:T(8,128)(2,1)S(1)}, u32[]{:S(2)}, u32[]{:S(2)}) collective-permute-start(bf16[1024,128]{1,0:T(8,128)(2,1)} %param.6), channel_id=1, source_target_pairs={{1,0},{2,1},{3,2},{4,3},{5,4},{6,5},{7,6},{8,7},{9,8},{10,9},{11,1... | collective-permute-start | bytes 786440 | tf_op jit(solution)/shard_map/ppermute | solution.py:22
  3.3 22.9 %collective-permute-start = (bf16[1024,128]{1,0:T(8,128)(2,1)}, bf16[1024,128]{1,0:T(8,128)(2,1)S(1)}, u32[]{:S(2)}, u32[]{:S(2)}) collective-permute-start(bf16[1024,128]{1,0:T(8,128)(2,1)} %param.6), channel_id=1, source_target_pairs={{0,1},{1,2},{2,3},{3,4},{4,5},{5,6},{6,7},{7,8},{8,9},{9,10},{10,1... | collective-permute-start | bytes 786440 | tf_op jit(solution)/shard_map/ppermute | solution.py:20
  6.5 3.6 %copy-start.2 = (bf16[1024,128]{1,0:T(8,128)(2,1)S(1)}, bf16[1024,128]{1,0:T(8,128)(2,1)}, u32[]{:S(2)}) copy-start(bf16[1024,128]{1,0:T(8,128)(2,1)} %param.6) | copy-start | bytes 786436
  15.1 22.8 %all-to-all-start = ((f32[16,128,128]{2,1,0:T(8,128)}), f32[16,128,128]{2,1,0:T(8,128)S(1)}, u32[]{:S(2)}, u32[]{:S(2)}) async-start(f32[16,128,128]{2,1,0:T(8,128)} %bitcast.8), calls=%async_computation | async-start | bytes 2097152 | tf_op jit(solution)/shard_map/all_to_all | solution.py:98
  22.7 3.4 %copy-start.3 = (s32[8,5]{1,0:T(8,128)S(1)}, s32[8,5]{1,0:T(8,128)}, u32[]{:S(2)}) copy-start(s32[8,5]{1,0:T(8,128)} %param.7) | copy-start | bytes 484
  46.9 3.8 %copy-start.4 = (f32[128,1024]{1,0:T(8,128)S(1)}, f32[128,1024]{1,0:T(8,128)}, u32[]{:S(2)}) copy-start(f32[128,1024]{1,0:T(8,128)} %fusion) | copy-start | bytes 1572868
  50.7 13.2 %copy-start.1 = (bf16[5120,128]{1,0:T(8,128)(2,1)S(1)}, bf16[5120,128]{1,0:T(8,128)(2,1)}, u32[]{:S(2)}) copy-start(bf16[5120,128]{1,0:T(8,128)(2,1)} %reshape.64) | copy-start | bytes 3932164
  54.6 9.9 %copy-start = (bf16[1,1024,640]{2,1,0:T(8,128)(2,1)S(1)}, bf16[1,1024,640]{2,1,0:T(8,128)(2,1)}, u32[]{:S(2)}) copy-start(bf16[1,1024,640]{2,1,0:T(8,128)(2,1)} %get-tuple-element.13) | copy-start | bytes 3932164
  55.4 18.1 %all-to-all-start.1 = ((f32[8,128,128]{1,2,0:T(8,128)}), f32[8,128,128]{1,2,0:T(8,128)}, u32[]{:S(2)}, u32[]{:S(2)}) async-start(f32[8,128,128]{1,2,0:T(8,128)} %bitcast.110), calls=%async_computation.1 | async-start | bytes 1048576 | tf_op jit(solution)/shard_map/all_to_all | solution.py:103
where the time goes:
time: 86.6 us; the launch traced here: 85.9 us
  matrix products  38.5 us (44%)
  starting transfers between devices  22.6 us (26%)
  waiting for transfers between devices  13.6 us (16%)
  local copies, waits for them, and re-layouts  10.2 us (12%)
    dot_general x4, matrix products, multiply_flat(): jnp.dot(imag_part, turned, preferred_element_type=jnp.float32)  13.8 us
    dot_general x4, matrix products, multiply_flat(): summed = jnp.dot(real_part, flat_data, preferred_element_type=jnp.float32)  12.5 us
    all_to_all x1, starting transfers between devices, on_device(): lax.all_to_all(middle, 'col', split_axis=0, concat_axis=0, tiled=True)  8.52 us
    all_to_all x1, waiting for transfers between devices, on_device(): lax.all_to_all(middle, 'col', split_axis=0, concat_axis=0, tiled=True)  8.36 us
    all_to_all x1, starting transfers between devices, on_device(): lax.all_to_all(shaped, 'row', split_axis=0, concat_axis=0, tiled=True)  7.6 us
    all_to_all x1, waiting for transfers between devices, on_device(): lax.all_to_all(shaped, 'row', split_axis=0, concat_axis=0, tiled=True)  5.23 us
    dot_general x1, matrix products, project_flat(): lax.dot_general(imag_part, turned, contract_dims, preferred_element_type=...  4.96 us
    dot_general x1, matrix products, project_flat(): lax.dot_general(real_part, flat_data, contract_dims, preferred_element_ty...  3.54 us
  transfers between devices with their start and end apart: 4, of which 2 were waited for; matrix products, arithmetic and copies ran while one was open for 23% of the time, Pallas kernels for 0%

commit v1 on v0

v1 whole, which is shorter than its diff:
```python
import functools

import jax
import jax.numpy as jnp
from jax import lax
from jax.experimental import pallas as pl
from jax.experimental.pallas import tpu as pltpu
from jax.sharding import PartitionSpec as P

RANK = 128
LEAF = 128
NEAR = 5
MESH = pl.DeviceIdType.MESH
BF16 = jnp.bfloat16
F32 = jnp.float32


def ring_order(count):
    return sorted(range(count), key=lambda k: (-min(k, count - k), k))


def turn(data):
    half = data.shape[1] // 2
    wide = data.astype(F32)
    rolled = pltpu.roll(wide, half, 1)
    lane = lax.broadcasted_iota(jnp.int32, wide.shape, 1)
    return jnp.where(lane < half, -rolled, rolled).astype(BF16)


def dot(a, b):
    return jnp.dot(a, b, preferred_element_type=F32)


def kernel(
    nx, nz, ny, nc,
    x_hbm, list_ref, near_hbm, col_hbm, mid_hbm, row_hbm, out_ref,
    table, turned, near, col, mid, row, xt, csend, arrived, tz, acc, msend, landed, far,
    x_sem, near_sem, col_sem, mid_sem, row_sem,
    halo_send, halo_recv, a_send, a_recv, b_send, b_recv,
):
    leaves = x_hbm.shape[0]
    unk = leaves * LEAF
    my_row, my_col = lax.axis_index("row"), lax.axis_index("col")
    x, z = my_row // nz, my_row % nz
    y, core = my_col // nc, my_col % nc
    n_col, n_all = ny * nc, nx * nz * ny * nc
    x_offs, z_offs, y_offs, c_offs = (ring_order(n) for n in (nx, nz, ny, nc))
    wx, wy = nz * RANK, nc * RANK

    me = my_row * n_col + my_col
    after = (me + 1) % n_all
    before = (me + n_all - 1) % n_all
    after_id = (after // n_col, after % n_col)
    before_id = (before // n_col, before % n_col)

    own = table.at[pl.ds(leaves, leaves)]
    load_x = pltpu.make_async_copy(x_hbm, own, x_sem)
    load_x.start()

    def span(position, width):
        return pl.ds(pl.multiple_of(position * width, width), width)

    load_col = [
        pltpu.make_async_copy(col_hbm.at[:, :, span((x + off) % nx, wx)], col.at[s], col_sem.at[s])
        for s, off in enumerate(x_offs)
    ]
    load_mid = [
        pltpu.make_async_copy(mid_hbm.at[:, :, span((x + nx - off) % nx, wx)], mid.at[s], mid_sem.at[s])
        for s, off in enumerate(x_offs)
    ]
    load_row = [
        pltpu.make_async_copy(row_hbm.at[:, :, span((y + ny - off) % ny, wy)], row.at[t], row_sem.at[t])
        for t, off in enumerate(y_offs)
    ]
    load_near = pltpu.make_async_copy(near_hbm, near, near_sem)
    for copy in load_col:
        copy.start()

    barrier = pltpu.get_barrier_semaphore()
    greeted = 0
    for off_x in range(nx):
        for off_z in range(nz):
            if off_x or off_z:
                peer = ((x + off_x) % nx * nz + (z + off_z) % nz, my_col)
                pl.semaphore_signal(barrier, inc=1, device_id=peer, device_id_type=MESH)
                greeted += 1
    for off in range(1, n_col):
        pl.semaphore_signal(barrier, inc=1, device_id=(my_row, (my_col + off) % n_col), device_id_type=MESH)
        greeted += 1
    for peer in (after_id, before_id):
        pl.semaphore_signal(barrier, inc=1, device_id=peer, device_id_type=MESH)
        greeted += 1
    pl.semaphore_wait(barrier, greeted)

    halo = [
        pltpu.make_async_remote_copy(
            x_hbm, table.at[pl.ds(0, leaves)], halo_send.at[0], halo_recv.at[0],
            device_id=after_id, device_id_type=MESH,
        ),
        pltpu.make_async_remote_copy(
            x_hbm, table.at[pl.ds(2 * leaves, leaves)], halo_send.at[1], halo_recv.at[1],
            device_id=before_id, device_id_type=MESH,
        ),
    ]
    for copy in halo:
        copy.start()

    load_x.wait()
    mine = table[pl.ds(leaves, leaves)].reshape(unk, LEAF)
    flipped = mine.astype(F32).T.astype(BF16)
    half = flipped.shape[0] // 2
    xt[0] = flipped
    xt[1] = jnp.concatenate([-flipped[half:], flipped[:half]], axis=0)
    turned[pl.ds(leaves, leaves)] = turn(mine).reshape(leaves, LEAF, LEAF)

    later = [[load_near], load_mid[:1], load_mid[1:2], load_mid[2:]]
    a_copies = []
    for s, off_x in enumerate(x_offs):
        load_col[s].wait()
        for copy in later[s] if s < len(later) else ():
            copy.start()
        block = dot(xt[0], col[s, 0]) + dot(xt[1], col[s, 1])
        for j in range(nz):
            csend[s, j] = block[:, j * RANK : (j + 1) * RANK].T.astype(BF16)
        for off_z in z_offs:
            to_z = (z + off_z) % nz
            if off_x == 0 and off_z == 0:
                arrived[s, pl.ds(pl.multiple_of(z * RANK, RANK), RANK), :] = csend[s, z]
                continue
            copy = pltpu.make_async_remote_copy(
                csend.at[s, to_z],
                arrived.at[s, pl.ds(pl.multiple_of(z * RANK, RANK), RANK)],
                a_send.at[s, to_z],
                a_recv.at[s, z],
                device_id=((x + off_x) % nx * nz + to_z, my_col),
                device_id_type=MESH,
            )
            copy.start()
            a_copies.append(copy)
    for copies in later[len(x_offs) :]:
        for copy in copies:
            copy.start()
    for copy in load_row:
        copy.start()

    for copy in halo:
        copy.wait_recv()
    load_near.wait()
    for start in (0, 2 * leaves):
        side = table[pl.ds(start, leaves)].reshape(unk, LEAF)
        turned[pl.ds(start, leaves)] = turn(side).reshape(leaves, LEAF, LEAF)
    first = me * leaves - leaves
    for i in range(leaves):
        total = None
        rows = pl.ds(i * LEAF, LEAF)
        for j in range(NEAR):
            place = jnp.clip(list_ref[i, j] - first, 0, 3 * leaves - 1)
            cols = pl.ds(j * LEAF, LEAF)
            part = dot(near[0, rows, cols], table[place]) + dot(near[1, rows, cols], turned[place])
            total = part if total is None else total + part
        far[rows, :] = total

    def arrivals(s, off_x):
        for off_z in z_offs:
            if off_x == 0 and off_z == 0:
                continue
            from_z = (z + nz - off_z) % nz
            slot = arrived.at[s, pl.ds(pl.multiple_of(from_z * RANK, RANK), RANK)]
            pltpu.make_async_copy(slot, slot, a_recv.at[s, from_z]).wait()
        load_mid[s].wait()
        tz[...] = turn(arrived[s])

    b_copies = []
    tile = nc * RANK
    for s, off_x in enumerate(x_offs):
        arrivals(s, off_x)
        for t, off_y in enumerate(y_offs):
            to_y = (y + off_y) % ny
            rows = pl.ds(pl.multiple_of(to_y * tile, tile), tile)
            part = dot(mid[s, 0, rows, :], arrived[s]) + dot(mid[s, 1, rows, :], tz[...])
            if s > 0:
                part = part + acc[t]
            if s < nx - 1:
                acc[t] = part
                continue
            msend[t] = part.astype(BF16)
            here = pl.ds(pl.multiple_of(core * RANK, RANK), RANK)
            for off_c in c_offs:
                to_c = (core + off_c) % nc
                there = pl.ds(pl.multiple_of(to_c * RANK, RANK), RANK)
                if off_y == 0 and off_c == 0:
                    landed[t, here, :] = msend[t, here, :]
                    continue
                copy = pltpu.make_async_remote_copy(
                    msend.at[t, there],
                    landed.at[t, here],
                    b_send.at[t, to_c],
                    b_recv.at[t, core],
                    device_id=(my_row, to_y * nc + to_c),
                    device_id_type=MESH,
                )
                copy.start()
                b_copies.append(copy)

    order = [ny - 1] + list(range(1, ny - 1)) + [0]
    for place, t in enumerate(order):
        for off_c in c_offs:
            if y_offs[t] == 0 and off_c == 0:
                continue
            from_c = (core + nc - off_c) % nc
            slot = landed.at[t, pl.ds(pl.multiple_of(from_c * RANK, RANK), RANK)]
            pltpu.make_async_copy(slot, slot, b_recv.at[t, from_c]).wait()
        load_row[t].wait()
        data = landed[t]
        part = far[...] + dot(row[t, 0], data) + dot(row[t, 1], turn(data))
        if place < ny - 1:
            far[...] = part
        else:
            out_ref[...] = part.astype(BF16)

    for copy in halo + a_copies + b_copies:
        copy.wait_send()


def on_device(sizes, excitation, near_list, near_blocks, col_factors, coupling, row_factors):
    nx, nz, ny, nc = sizes
    unk, cols = excitation.shape
    dma = pltpu.SemaphoreType.DMA
    hbm = pl.BlockSpec(memory_space=pl.ANY)
    rows_mid = coupling.shape[1]
    moved = sum(a.size * 2 for a in (near_blocks, col_factors, coupling, row_factors))
    return pl.pallas_call(
        functools.partial(kernel, nx, nz, ny, nc),
        out_shape=jax.ShapeDtypeStruct((unk, cols), BF16),
        in_specs=[hbm, pl.BlockSpec(memory_space=pltpu.SMEM), hbm, hbm, hbm, hbm],
        out_specs=pl.BlockSpec(memory_space=pltpu.VMEM),
        scratch_shapes=[
            pltpu.VMEM((3 * unk // LEAF, LEAF, cols), BF16),
            pltpu.VMEM((3 * unk // LEAF, LEAF, cols), BF16),
            pltpu.VMEM(near_blocks.shape, BF16),
            pltpu.VMEM((nx, 2, unk, nz * RANK), BF16),
            pltpu.VMEM((nx, 2, rows_mid, nz * RANK), BF16),
            pltpu.VMEM((ny, 2, unk, nc * RANK), BF16),
            pltpu.VMEM((2, cols, unk), BF16),
            pltpu.VMEM((nx, nz, RANK, cols), BF16),
            pltpu.VMEM((nx, nz * RANK, cols), BF16),
            pltpu.VMEM((nz * RANK, cols), BF16),
            pltpu.VMEM((ny, nc * RANK, cols), F32),
            pltpu.VMEM((ny, nc * RANK, cols), BF16),
            pltpu.VMEM((ny, nc * RANK, cols), BF16),
            pltpu.VMEM((unk, cols), F32),
            dma, dma, dma((nx,)), dma((nx,)), dma((ny,)),
            dma((2,)), dma((2,)), dma((nx, nz)), dma((nx, nz)), dma((ny, nc)), dma((ny, nc)),
        ],
        compiler_params=pltpu.CompilerParams(
            collective_id=0, has_side_effects=True, vmem_limit_bytes=56 * 2**20
        ),
        cost_estimate=pl.CostEstimate(flops=128 * moved, bytes_accessed=moved, transcendentals=0),
    )(excitation.reshape(unk // LEAF, LEAF, cols), near_list, near_blocks, col_factors, coupling, row_factors)


def solution(mesh):
    nx = nz = int(round(mesh.shape["row"] ** 0.5))
    nc = 2
    ny = mesh.shape["col"] // nc
    split = P(("row", "col"), None)
    split3 = P(None, ("row", "col"), None)
    return jax.shard_map(
        functools.partial(on_device, (nx, nz, ny, nc)),
        mesh=mesh,
        in_specs=(split, split, split3, split3, split3, split3),
        out_specs=split,
        check_vma=False,
    )
```

time: 86.6 us -> 32.1 us (0.37)
  matrix products: 38.5 us -> 0 us
  Pallas kernels: 0 us -> 30.2 us
  starting transfers between devices: 22.6 us -> 0 us
  waiting for transfers between devices: 13.6 us -> 0 us
  local copies, waits for them, and re-layouts: 10.2 us -> 1.67 us
    dot_general x14 -> x0, matrix products: 38.5 us -> none  [the longest x4 13.8 us: multiply_flat(): jnp.dot(imag_part, turned, preferred_element_type=jnp.float32)]
    pallas_call x0 -> x1, Pallas kernels: none -> 30.2 us  [on_device(): pl.pallas_call(functools.partial(kernel, nx, nz, ny, nc), out_shape=jax.S...]
    all_to_all x2 -> x0, starting transfers between devices: 16.1 us -> none  [the longest x1 8.52 us: on_device(): lax.all_to_all(middle, 'col', split_axis=0, concat_axis=0, tiled=True)]
    all_to_all x2 -> x0, waiting for transfers between devices: 13.6 us -> none  [the longest x1 8.36 us: on_device(): lax.all_to_all(middle, 'col', split_axis=0, concat_axis=0, tiled=True)]
    ppermute x2 -> x0, starting transfers between devices: 6.51 us -> none  [the longest x1 3.32 us: with_halo(): lax.ppermute(head, axis, [((i + 1) % count, i) for i in range(ends)])]
    slice x1 -> x0, local copies, waits for them, and re-layouts: 3.4 us -> none  [on_device(): blocks_im = near_blocks[1].reshape(leaves_here, LEAF, NEAR * LEAF)]
    reshape x4 -> x0, local copies, waits for them, and re-layouts: 3.03 us -> none  [the longest x1 1.67 us: on_device(): pieces = pieces.reshape(leaves_here * NEAR * LEAF, width_cols)]
    another operation x1 -> x0, local copies, waits for them, and re-layouts: 1.66 us -> none  [on_device(): pieces = pieces.reshape(leaves_here, NEAR * LEAF, width_cols)]
  transfers between devices with their start and end apart: 4 -> 0, of which waited for: 2 -> 0; matrix products, arithmetic and copies ran while one was open for 23% -> 0% of each run, Pallas kernels for 0% -> 0%
where the time goes in v1:
time: 32.1 us; the launch traced here: 31.9 us
  Pallas kernels  30.2 us (94%)
  local copies, waits for them, and re-layouts  1.67 us (5%)
    pallas_call x1, Pallas kernels, on_device(): pl.pallas_call(functools.partial(kernel, nx, nz, ny, nc), out_shape=jax.S...  30.2 us
    unnamed x1, local copies, waits for them, and re-layouts  1.67 us

profile of v1, /device:TPU:1, one launch (start us, length us, event | category | flops | bytes accessed | tf_op | source)
XLA Modules:
  0.0 31.9 jit_solution(204624743911565697)
XLA Ops:
  0.0 30.2 %shard_map.64 = bf16[1024,128]{1,0:T(8,128)(2,1)} custom-call(bf16[8,128,128]{2,1,0:T(8,128)(2,1)} %bitcast.1, s32[8,5]{1,0:T(8,128)} %list_ref.1, bf16[2,1024,640]{2,1,0:T(8,128)(2,1)} %near_hbm.1, bf16[2,1024,2048]{2,1,0:T(8,128)(2,1)} %col_hbm.1, bf16[2,1024,2048]{2,1,0:T(8,128)(2,1)} %mid_hbm.1, bf16[2,1024,1024]{2,1,0:T(8,128)(2,1)} %row_hbm.1), custom_call_target="tpu_custom_call" | custom-call | flops 3019898880 | bytes 23592960 | tf_op jit(solution)/shard_map/pallas_call | solution.py:232
  30.2 1.7 %copy.8 = bf16[1024,128]{1,0:T(8,128)(2,1)} copy(bf16[1024,128]{1,0:T(8,128)(2,1)} %shard_map.64) | data formatting | bytes 524288

commit v2 on v1

--- a/solution.py
+++ b/solution.py
@@ -90,20 +90,6 @@
     for peer in (after_id, before_id):
         pl.semaphore_signal(barrier, inc=1, device_id=peer, device_id_type=MESH)
         greeted += 1
-    pl.semaphore_wait(barrier, greeted)
-
-    halo = [
-        pltpu.make_async_remote_copy(
-            x_hbm, table.at[pl.ds(0, leaves)], halo_send.at[0], halo_recv.at[0],
-            device_id=after_id, device_id_type=MESH,
-        ),
-        pltpu.make_async_remote_copy(
-            x_hbm, table.at[pl.ds(2 * leaves, leaves)], halo_send.at[1], halo_recv.at[1],
-            device_id=before_id, device_id_type=MESH,
-        ),
-    ]
-    for copy in halo:
-        copy.start()
 
     load_x.wait()
     mine = table[pl.ds(leaves, leaves)].reshape(unk, LEAF)
@@ -122,6 +108,8 @@
         block = dot(xt[0], col[s, 0]) + dot(xt[1], col[s, 1])
         for j in range(nz):
             csend[s, j] = block[:, j * RANK : (j + 1) * RANK].T.astype(BF16)
+        if s == 0:
+            pl.semaphore_wait(barrier, greeted)
         for off_z in z_offs:
             to_z = (z + off_z) % nz
             if off_x == 0 and off_z == 0:
@@ -143,22 +131,18 @@
     for copy in load_row:
         copy.start()
 
+    halo = [
+        pltpu.make_async_remote_copy(
+            x_hbm, table.at[pl.ds(0, leaves)], halo_send.at[0], halo_recv.at[0],
+            device_id=after_id, device_id_type=MESH,
+        ),
+        pltpu.make_async_remote_copy(
+            x_hbm, table.at[pl.ds(2 * leaves, leaves)], halo_send.at[1], halo_recv.at[1],
+            device_id=before_id, device_id_type=MESH,
+        ),
+    ]
     for copy in halo:
-        copy.wait_recv()
-    load_near.wait()
-    for start in (0, 2 * leaves):
-        side = table[pl.ds(start, leaves)].reshape(unk, LEAF)
-        turned[pl.ds(start, leaves)] = turn(side).reshape(leaves, LEAF, LEAF)
-    first = me * leaves - leaves
-    for i in range(leaves):
-        total = None
-        rows = pl.ds(i * LEAF, LEAF)
-        for j in range(NEAR):
-            place = jnp.clip(list_ref[i, j] - first, 0, 3 * leaves - 1)
-            cols = pl.ds(j * LEAF, LEAF)
-            part = dot(near[0, rows, cols], table[place]) + dot(near[1, rows, cols], turned[place])
-            total = part if total is None else total + part
-        far[rows, :] = total
+        copy.start()
 
     def arrivals(s, off_x):
         for off_z in z_offs:
@@ -202,8 +186,24 @@
                 copy.start()
                 b_copies.append(copy)
 
-    order = [ny - 1] + list(range(1, ny - 1)) + [0]
-    for place, t in enumerate(order):
+    for copy in halo:
+        copy.wait_recv()
+    load_near.wait()
+    for start in (0, 2 * leaves):
+        side = table[pl.ds(start, leaves)].reshape(unk, LEAF)
+        turned[pl.ds(start, leaves)] = turn(side).reshape(leaves, LEAF, LEAF)
+    first = me * leaves - leaves
+    for i in range(leaves):
+        total = None
+        rows = pl.ds(i * LEAF, LEAF)
+        for j in range(NEAR):
+            place = jnp.clip(list_ref[i, j] - first, 0, 3 * leaves - 1)
+            cols = pl.ds(j * LEAF, LEAF)
+            part = dot(near[0, rows, cols], table[place]) + dot(near[1, rows, cols], turned[place])
+            total = part if total is None else total + part
+        far[rows, :] = total
+
+    for t in range(ny):
         for off_c in c_offs:
             if y_offs[t] == 0 and off_c == 0:
                 continue
@@ -211,15 +211,22 @@
             slot = landed.at[t, pl.ds(pl.multiple_of(from_c * RANK, RANK), RANK)]
             pltpu.make_async_copy(slot, slot, b_recv.at[t, from_c]).wait()
         load_row[t].wait()
-        data = landed[t]
-        part = far[...] + dot(row[t, 0], data) + dot(row[t, 1], turn(data))
-        if place < ny - 1:
-            far[...] = part
-        else:
-            out_ref[...] = part.astype(BF16)
+    turns = [turn(landed[t]) for t in range(ny)]
+    for i in range(unk // 1024):
+        rows = pl.ds(i * 1024, 1024)
+        part = far[rows, :]
+        for t in range(ny):
+            part = part + dot(row[t, 0, rows, :], landed[t]) + dot(row[t, 1, rows, :], turns[t])
+        out_ref[rows, :] = part.astype(BF16)
 
     for copy in halo + a_copies + b_copies:
         copy.wait_send()
+
+
+def put_out(data_ref, out_ref, sem):
+    copy = pltpu.make_async_copy(data_ref, out_ref, sem)
+    copy.start()
+    copy.wait()
 
 
 def on_device(sizes, excitation, near_list, near_blocks, col_factors, coupling, row_factors):
@@ -229,9 +236,9 @@
     hbm = pl.BlockSpec(memory_space=pl.ANY)
     rows_mid = coupling.shape[1]
     moved = sum(a.size * 2 for a in (near_blocks, col_factors, coupling, row_factors))
-    return pl.pallas_call(
+    response = pl.pallas_call(
         functools.partial(kernel, nx, nz, ny, nc),
-        out_shape=jax.ShapeDtypeStruct((unk, cols), BF16),
+        out_shape=pltpu.VMEM((unk, cols), BF16),
         in_specs=[hbm, pl.BlockSpec(memory_space=pltpu.SMEM), hbm, hbm, hbm, hbm],
         out_specs=pl.BlockSpec(memory_space=pltpu.VMEM),
         scratch_shapes=[
@@ -257,6 +264,7 @@
         ),
         cost_estimate=pl.CostEstimate(flops=128 * moved, bytes_accessed=moved, transcendentals=0),
     )(excitation.reshape(unk // LEAF, LEAF, cols), near_list, near_blocks, col_factors, coupling, row_factors)
+    return response
 
 
 def solution(mesh):

time: 32.1 us -> 27.5 us (0.86)
  Pallas kernels: 30.2 us -> 26.6 us
  local copies, waits for them, and re-layouts: 1.67 us -> 0.71 us
    pallas_call x1, Pallas kernels: 30.2 us -> 26.6 us  [on_device(): pl.pallas_call(functools.partial(kernel, nx, nz, ny, nc), out_shape=pltpu...]
    unnamed x1, local copies, waits for them, and re-layouts: 1.67 us -> 0.71 us
where the time goes in v2:
time: 27.5 us; the launch traced here: 27.4 us
  Pallas kernels  26.6 us (97%)
  local copies, waits for them, and re-layouts  0.71 us (3%)
    pallas_call x1, Pallas kernels, on_device(): pl.pallas_call(functools.partial(kernel, nx, nz, ny, nc), out_shape=pltpu...  26.6 us
    unnamed x1, local copies, waits for them, and re-layouts  0.71 us

profile of v2, /device:TPU:1, one launch (start us, length us, event | category | flops | bytes accessed | tf_op | source)
XLA Modules:
  0.0 27.4 jit_solution(13885968827856065400)
XLA Ops:
  0.0 26.6 %shard_map.64 = bf16[1024,128]{1,0:T(8,128)(2,1)S(1)} custom-call(bf16[8,128,128]{2,1,0:T(8,128)(2,1)} %bitcast.1, s32[8,5]{1,0:T(8,128)} %list_ref.1, bf16[2,1024,640]{2,1,0:T(8,128)(2,1)} %near_hbm.1, bf16[2,1024,2048]{2,1,0:T(8,128)(2,1)} %col_hbm.1, bf16[2,1024,2048]{2,1,0:T(8,128)(2,1)} %mid_hbm.1, bf16[2,1024,1024]{2,1,0:T(8,128)(2,1)} %row_hbm.1), custom_call_target="tpu_custom_call" | custom-call | flops 3019898880 | bytes 23592960 | tf_op jit(solution)/shard_map/pallas_call | solution.py:239
  26.6 0.7 %copy.8 = bf16[1024,128]{1,0:T(8,128)(2,1)} copy(bf16[1024,128]{1,0:T(8,128)(2,1)S(1)} %shard_map.64) | data formatting | bytes 524288

commit v3 on v2

--- a/solution.py
+++ b/solution.py
@@ -33,9 +33,9 @@
 
 def kernel(
     nx, nz, ny, nc,
-    x_hbm, list_ref, near_hbm, col_hbm, mid_hbm, row_hbm, out_ref,
-    table, turned, near, col, mid, row, xt, csend, arrived, tz, acc, msend, landed, far,
-    x_sem, near_sem, col_sem, mid_sem, row_sem,
+    x_hbm, list_hbm, near_hbm, col_hbm, mid_hbm, row_hbm, out_ref,
+    list_ref, table, turned, near, col, mid, row, xt, csend, arrived, tz, acc, msend, landed, far,
+    list_sem, x_sem, near_sem, col_sem, mid_sem, row_sem,
     halo_send, halo_recv, a_send, a_recv, b_send, b_recv,
 ):
     leaves = x_hbm.shape[0]
@@ -97,9 +97,9 @@
     half = flipped.shape[0] // 2
     xt[0] = flipped
     xt[1] = jnp.concatenate([-flipped[half:], flipped[:half]], axis=0)
-    turned[pl.ds(leaves, leaves)] = turn(mine).reshape(leaves, LEAF, LEAF)
-
-    later = [[load_near], load_mid[:1], load_mid[1:2], load_mid[2:]]
+
+    load_list = pltpu.make_async_copy(list_hbm, list_ref, list_sem)
+    later = [[load_list, load_near], load_mid[:1], load_mid[1:2], load_mid[2:]]
     a_copies = []
     for s, off_x in enumerate(x_offs):
         load_col[s].wait()
@@ -189,7 +189,8 @@
     for copy in halo:
         copy.wait_recv()
     load_near.wait()
-    for start in (0, 2 * leaves):
+    load_list.wait()
+    for start in (0, leaves, 2 * leaves):
         side = table[pl.ds(start, leaves)].reshape(unk, LEAF)
         turned[pl.ds(start, leaves)] = turn(side).reshape(leaves, LEAF, LEAF)
     first = me * leaves - leaves
@@ -203,7 +204,7 @@
             total = part if total is None else total + part
         far[rows, :] = total
 
-    for t in range(ny):
+    def landing(t):
         for off_c in c_offs:
             if y_offs[t] == 0 and off_c == 0:
                 continue
@@ -211,13 +212,15 @@
             slot = landed.at[t, pl.ds(pl.multiple_of(from_c * RANK, RANK), RANK)]
             pltpu.make_async_copy(slot, slot, b_recv.at[t, from_c]).wait()
         load_row[t].wait()
-    turns = [turn(landed[t]) for t in range(ny)]
-    for i in range(unk // 1024):
-        rows = pl.ds(i * 1024, 1024)
-        part = far[rows, :]
-        for t in range(ny):
-            part = part + dot(row[t, 0, rows, :], landed[t]) + dot(row[t, 1, rows, :], turns[t])
-        out_ref[rows, :] = part.astype(BF16)
+
+    landing(ny - 1)
+    far[...] += dot(row[ny - 1, 0], landed[ny - 1]) + dot(row[ny - 1, 1], turn(landed[ny - 1]))
+    for t in range(ny - 1):
+        landing(t)
+    part = far[...]
+    for t in range(ny - 1):
+        part = part + dot(row[t, 0], landed[t]) + dot(row[t, 1], turn(landed[t]))
+    out_ref[...] = part.astype(BF16)
 
     for copy in halo + a_copies + b_copies:
         copy.wait_send()
@@ -239,9 +242,10 @@
     response = pl.pallas_call(
         functools.partial(kernel, nx, nz, ny, nc),
         out_shape=pltpu.VMEM((unk, cols), BF16),
-        in_specs=[hbm, pl.BlockSpec(memory_space=pltpu.SMEM), hbm, hbm, hbm, hbm],
+        in_specs=[hbm, hbm, hbm, hbm, hbm, hbm],
         out_specs=pl.BlockSpec(memory_space=pltpu.VMEM),
         scratch_shapes=[
+            pltpu.SMEM(near_list.shape, jnp.int32),
             pltpu.VMEM((3 * unk // LEAF, LEAF, cols), BF16),
             pltpu.VMEM((3 * unk // LEAF, LEAF, cols), BF16),
             pltpu.VMEM(near_blocks.shape, BF16),
@@ -256,7 +260,7 @@
             pltpu.VMEM((ny, nc * RANK, cols), BF16),
             pltpu.VMEM((ny, nc * RANK, cols), BF16),
             pltpu.VMEM((unk, cols), F32),
-            dma, dma, dma((nx,)), dma((nx,)), dma((ny,)),
+            dma, dma, dma, dma((nx,)), dma((nx,)), dma((ny,)),
             dma((2,)), dma((2,)), dma((nx, nz)), dma((nx, nz)), dma((ny, nc)), dma((ny, nc)),
         ],
         compiler_params=pltpu.CompilerParams(

time: 27.5 us -> 26.6 us (0.967)
  Pallas kernels: 26.6 us -> 25.8 us
    pallas_call x1, Pallas kernels: 26.6 us -> 25.8 us  [on_device(): pl.pallas_call(functools.partial(kernel, nx, nz, ny, nc), out_shape=pltpu...]
where the time goes in v3:
time: 26.6 us; the launch traced here: 26.5 us
  Pallas kernels  25.8 us (97%)
  local copies, waits for them, and re-layouts  0.71 us (3%)
    pallas_call x1, Pallas kernels, on_device(): pl.pallas_call(functools.partial(kernel, nx, nz, ny, nc), out_shape=pltpu...  25.8 us
    unnamed x1, local copies, waits for them, and re-layouts  0.71 us

profile of v3, /device:TPU:1, one launch (start us, length us, event | category | flops | bytes accessed | tf_op | source)
XLA Modules:
  0.0 26.5 jit_solution(10076231419126473838)
XLA Ops:
  0.0 25.8 %shard_map.64 = bf16[1024,128]{1,0:T(8,128)(2,1)S(1)} custom-call(bf16[8,128,128]{2,1,0:T(8,128)(2,1)} %bitcast.1, s32[8,5]{1,0:T(8,128)} %list_hbm.1, bf16[2,1024,640]{2,1,0:T(8,128)(2,1)} %near_hbm.1, bf16[2,1024,2048]{2,1,0:T(8,128)(2,1)} %col_hbm.1, bf16[2,1024,2048]{2,1,0:T(8,128)(2,1)} %mid_hbm.1, bf16[2,1024,1024]{2,1,0:T(8,128)(2,1)} %row_hbm.1), custom_call_target="tpu_custom_call" | custom-call | flops 3019898880 | bytes 23592960 | tf_op jit(solution)/shard_map/pallas_call | solution.py:242
  25.8 0.7 %copy.8 = bf16[1024,128]{1,0:T(8,128)(2,1)} copy(bf16[1024,128]{1,0:T(8,128)(2,1)S(1)} %shard_map.64) | data formatting | bytes 524288

commit v4 on v3

--- a/solution.py
+++ b/solution.py
@@ -27,6 +27,15 @@
     return jnp.where(lane < half, -rolled, rolled).astype(BF16)
 
 
+def swap(data):
+    half = data.shape[0] // 2
+    return jnp.concatenate([-data[half:], data[:half]], axis=0)
+
+
+def dot_t(a, b):
+    return lax.dot_general(a, b, (((1,), (1,)), ((), ())), preferred_element_type=F32)
+
+
 def dot(a, b):
     return jnp.dot(a, b, preferred_element_type=F32)
 
@@ -34,7 +43,7 @@
 def kernel(
     nx, nz, ny, nc,
     x_hbm, list_hbm, near_hbm, col_hbm, mid_hbm, row_hbm, out_ref,
-    list_ref, table, turned, near, col, mid, row, xt, csend, arrived, tz, acc, msend, landed, far,
+    list_ref, table, turned, near, col, mid, row, xt, csend, arrived, mid_t, row_t, acc, msend, landed, far,
     list_sem, x_sem, near_sem, col_sem, mid_sem, row_sem,
     halo_send, halo_recv, a_send, a_recv, b_send, b_recv,
 ):
@@ -65,7 +74,14 @@
         for s, off in enumerate(x_offs)
     ]
     load_mid = [
-        pltpu.make_async_copy(mid_hbm.at[:, :, span((x + nx - off) % nx, wx)], mid.at[s], mid_sem.at[s])
+        [
+            pltpu.make_async_copy(
+                mid_hbm.at[:, span((y + off_y) % ny, wy), span((x + nx - off) % nx, wx)],
+                mid.at[s, :, pl.ds(t * wy, wy)],
+                mid_sem.at[s, t],
+            )
+            for t, off_y in enumerate(y_offs)
+        ]
         for s, off in enumerate(x_offs)
     ]
     load_row = [
@@ -99,7 +115,7 @@
     xt[1] = jnp.concatenate([-flipped[half:], flipped[:half]], axis=0)
 
     load_list = pltpu.make_async_copy(list_hbm, list_ref, list_sem)
-    later = [[load_list, load_near], load_mid[:1], load_mid[1:2], load_mid[2:]]
+    later = [load_mid[-1], load_row, [load_list, load_near] + load_mid[0], sum(load_mid[1:-1], [])]
     a_copies = []
     for s, off_x in enumerate(x_offs):
         load_col[s].wait()
@@ -107,17 +123,17 @@
             copy.start()
         block = dot(xt[0], col[s, 0]) + dot(xt[1], col[s, 1])
         for j in range(nz):
-            csend[s, j] = block[:, j * RANK : (j + 1) * RANK].T.astype(BF16)
+            csend[s, j] = block[:, j * RANK : (j + 1) * RANK].astype(BF16)
         if s == 0:
             pl.semaphore_wait(barrier, greeted)
         for off_z in z_offs:
             to_z = (z + off_z) % nz
             if off_x == 0 and off_z == 0:
-                arrived[s, pl.ds(pl.multiple_of(z * RANK, RANK), RANK), :] = csend[s, z]
+                arrived[s, z] = csend[s, z]
                 continue
             copy = pltpu.make_async_remote_copy(
                 csend.at[s, to_z],
-                arrived.at[s, pl.ds(pl.multiple_of(z * RANK, RANK), RANK)],
+                arrived.at[s, z],
                 a_send.at[s, to_z],
                 a_recv.at[s, z],
                 device_id=((x + off_x) % nx * nz + to_z, my_col),
@@ -128,8 +144,6 @@
     for copies in later[len(x_offs) :]:
         for copy in copies:
             copy.start()
-    for copy in load_row:
-        copy.start()
 
     halo = [
         pltpu.make_async_remote_copy(
@@ -144,40 +158,46 @@
     for copy in halo:
         copy.start()
 
-    def arrivals(s, off_x):
+    for copy in load_mid[-1]:
+        copy.wait()
+    for p in range(2):
+        mid_t[p] = mid[nx - 1, p].T
+    for t in range(ny):
+        load_row[t].wait()
+        for p in range(2):
+            row_t[t, p] = row[t, p].T
+
+    tile = wy
+    b_copies = []
+    for s, off_x in enumerate(x_offs):
         for off_z in z_offs:
             if off_x == 0 and off_z == 0:
                 continue
             from_z = (z + nz - off_z) % nz
-            slot = arrived.at[s, pl.ds(pl.multiple_of(from_z * RANK, RANK), RANK)]
+            slot = arrived.at[s, from_z]
             pltpu.make_async_copy(slot, slot, a_recv.at[s, from_z]).wait()
-        load_mid[s].wait()
-        tz[...] = turn(arrived[s])
-
-    b_copies = []
-    tile = nc * RANK
-    for s, off_x in enumerate(x_offs):
-        arrivals(s, off_x)
+        data = jnp.concatenate([arrived[s, j] for j in range(nz)], axis=1)
+        flip = swap(data)
+        if s < nx - 1:
+            for copy in load_mid[s]:
+                copy.wait()
+            part = dot_t(data, mid[s, 0]) + dot_t(flip, mid[s, 1])
+            acc[...] = part if s == 0 else acc[...] + part
+            continue
         for t, off_y in enumerate(y_offs):
             to_y = (y + off_y) % ny
-            rows = pl.ds(pl.multiple_of(to_y * tile, tile), tile)
-            part = dot(mid[s, 0, rows, :], arrived[s]) + dot(mid[s, 1, rows, :], tz[...])
-            if s > 0:
-                part = part + acc[t]
-            if s < nx - 1:
-                acc[t] = part
-                continue
-            msend[t] = part.astype(BF16)
-            here = pl.ds(pl.multiple_of(core * RANK, RANK), RANK)
+            rows = pl.ds(t * tile, tile)
+            part = acc[:, rows] + dot(data, mid_t[0, :, rows]) + dot(flip, mid_t[1, :, rows])
+            for q in range(nc):
+                msend[t, q] = part[:, q * RANK : (q + 1) * RANK].astype(BF16)
             for off_c in c_offs:
                 to_c = (core + off_c) % nc
-                there = pl.ds(pl.multiple_of(to_c * RANK, RANK), RANK)
                 if off_y == 0 and off_c == 0:
-                    landed[t, here, :] = msend[t, here, :]
+                    landed[t, core] = msend[t, core]
                     continue
                 copy = pltpu.make_async_remote_copy(
-                    msend.at[t, there],
-                    landed.at[t, here],
+                    msend.at[t, to_c],
+                    landed.at[t, core],
                     b_send.at[t, to_c],
                     b_recv.at[t, core],
                     device_id=(my_row, to_y * nc + to_c),
@@ -209,18 +229,23 @@
             if y_offs[t] == 0 and off_c == 0:
                 continue
             from_c = (core + nc - off_c) % nc
-            slot = landed.at[t, pl.ds(pl.multiple_of(from_c * RANK, RANK), RANK)]
+            slot = landed.at[t, from_c]
             pltpu.make_async_copy(slot, slot, b_recv.at[t, from_c]).wait()
-        load_row[t].wait()
+
+    def expand(t):
+        data = jnp.concatenate([landed[t, q] for q in range(nc)], axis=1)
+        return dot(data, row_t[t, 0]) + dot(swap(data), row_t[t, 1])
 
     landing(ny - 1)
-    far[...] += dot(row[ny - 1, 0], landed[ny - 1]) + dot(row[ny - 1, 1], turn(landed[ny - 1]))
+    part = expand(ny - 1)
+    for i in range(leaves):
+        far[pl.ds(i * LEAF, LEAF), :] += part[:, i * LEAF : (i + 1) * LEAF].T
     for t in range(ny - 1):
         landing(t)
-    part = far[...]
-    for t in range(ny - 1):
-        part = part + dot(row[t, 0], landed[t]) + dot(row[t, 1], turn(landed[t]))
-    out_ref[...] = part.astype(BF16)
+    part = sum(expand(t) for t in range(ny - 1))
+    for i in range(leaves):
+        rows = pl.ds(i * LEAF, LEAF)
+        out_ref[rows, :] = (far[rows, :] + part[:, i * LEAF : (i + 1) * LEAF].T).astype(BF16)
 
     for copy in halo + a_copies + b_copies:
         copy.wait_send()
@@ -253,14 +278,15 @@
             pltpu.VMEM((nx, 2, rows_mid, nz * RANK), BF16),
             pltpu.VMEM((ny, 2, unk, nc * RANK), BF16),
             pltpu.VMEM((2, cols, unk), BF16),
-            pltpu.VMEM((nx, nz, RANK, cols), BF16),
-            pltpu.VMEM((nx, nz * RANK, cols), BF16),
-            pltpu.VMEM((nz * RANK, cols), BF16),
-            pltpu.VMEM((ny, nc * RANK, cols), F32),
-            pltpu.VMEM((ny, nc * RANK, cols), BF16),
-            pltpu.VMEM((ny, nc * RANK, cols), BF16),
+            pltpu.VMEM((nx, nz, cols, RANK), BF16),
+            pltpu.VMEM((nx, nz, cols, RANK), BF16),
+            pltpu.VMEM((2, nz * RANK, rows_mid), BF16),
+            pltpu.VMEM((ny, 2, nc * RANK, unk), BF16),
+            pltpu.VMEM((cols, rows_mid), F32),
+            pltpu.VMEM((ny, nc, cols, RANK), BF16),
+            pltpu.VMEM((ny, nc, cols, RANK), BF16),
             pltpu.VMEM((unk, cols), F32),
-            dma, dma, dma, dma((nx,)), dma((nx,)), dma((ny,)),
+            dma, dma, dma, dma((nx,)), dma((nx, ny)), dma((ny,)),
             dma((2,)), dma((2,)), dma((nx, nz)), dma((nx, nz)), dma((ny, nc)), dma((ny, nc)),
         ],
         compiler_params=pltpu.CompilerParams(

time: 26.6 us -> 25.7 us (0.966)
  Pallas kernels: 25.8 us -> 24.9 us
    pallas_call x1, Pallas kernels: 25.8 us -> 24.9 us  [on_device(): pl.pallas_call(functools.partial(kernel, nx, nz, ny, nc), out_shape=pltpu...]
where the time goes in v4:
time: 25.7 us; the launch traced here: 25.6 us
  Pallas kernels  24.9 us (97%)
  local copies, waits for them, and re-layouts  0.71 us (3%)
    pallas_call x1, Pallas kernels, on_device(): pl.pallas_call(functools.partial(kernel, nx, nz, ny, nc), out_shape=pltpu...  24.9 us
    unnamed x1, local copies, waits for them, and re-layouts  0.71 us

profile of v4, /device:TPU:1, one launch (start us, length us, event | category | flops | bytes accessed | tf_op | source)
XLA Modules:
  0.0 25.6 jit_solution(13959704971037553963)
XLA Ops:
  0.0 24.9 %shard_map.64 = bf16[1024,128]{1,0:T(8,128)(2,1)S(1)} custom-call(bf16[8,128,128]{2,1,0:T(8,128)(2,1)} %bitcast.1, s32[8,5]{1,0:T(8,128)} %list_hbm.1, bf16[2,1024,640]{2,1,0:T(8,128)(2,1)} %near_hbm.1, bf16[2,1024,2048]{2,1,0:T(8,128)(2,1)} %col_hbm.1, bf16[2,1024,2048]{2,1,0:T(8,128)(2,1)} %mid_hbm.1, bf16[2,1024,1024]{2,1,0:T(8,128)(2,1)} %row_hbm.1), custom_call_target="tpu_custom_call" | custom-call | flops 3019898880 | bytes 23592960 | tf_op jit(solution)/shard_map/pallas_call | solution.py:267
  24.9 0.7 %copy.8 = bf16[1024,128]{1,0:T(8,128)(2,1)} copy(bf16[1024,128]{1,0:T(8,128)(2,1)S(1)} %shard_map.64) | data formatting | bytes 524288

commit v5 on v4

--- a/solution.py
+++ b/solution.py
@@ -145,19 +145,6 @@
         for copy in copies:
             copy.start()
 
-    halo = [
-        pltpu.make_async_remote_copy(
-            x_hbm, table.at[pl.ds(0, leaves)], halo_send.at[0], halo_recv.at[0],
-            device_id=after_id, device_id_type=MESH,
-        ),
-        pltpu.make_async_remote_copy(
-            x_hbm, table.at[pl.ds(2 * leaves, leaves)], halo_send.at[1], halo_recv.at[1],
-            device_id=before_id, device_id_type=MESH,
-        ),
-    ]
-    for copy in halo:
-        copy.start()
-
     for copy in load_mid[-1]:
         copy.wait()
     for p in range(2):
@@ -170,6 +157,19 @@
     tile = wy
     b_copies = []
     for s, off_x in enumerate(x_offs):
+        if s == 1:
+            halo = [
+                pltpu.make_async_remote_copy(
+                    x_hbm, table.at[pl.ds(0, leaves)], halo_send.at[0], halo_recv.at[0],
+                    device_id=after_id, device_id_type=MESH,
+                ),
+                pltpu.make_async_remote_copy(
+                    x_hbm, table.at[pl.ds(2 * leaves, leaves)], halo_send.at[1], halo_recv.at[1],
+                    device_id=before_id, device_id_type=MESH,
+                ),
+            ]
+            for copy in halo:
+                copy.start()
         for off_z in z_offs:
             if off_x == 0 and off_z == 0:
                 continue

time: 25.7 us -> 25.3 us (0.984)
  Pallas kernels: 24.9 us -> 24.5 us
    pallas_call x1, Pallas kernels: 24.9 us -> 24.5 us  [on_device(): pl.pallas_call(functools.partial(kernel, nx, nz, ny, nc), out_shape=pltpu...]
where the time goes in v5:
time: 25.3 us; the launch traced here: 25.2 us
  Pallas kernels  24.5 us (97%)
  local copies, waits for them, and re-layouts  0.71 us (3%)
    pallas_call x1, Pallas kernels, on_device(): pl.pallas_call(functools.partial(kernel, nx, nz, ny, nc), out_shape=pltpu...  24.5 us
    unnamed x1, local copies, waits for them, and re-layouts  0.71 us

profile of v5, /device:TPU:1, one launch (start us, length us, event | category | flops | bytes accessed | tf_op | source)
XLA Modules:
  0.0 25.2 jit_solution(3270802040864752461)
XLA Ops:
  0.0 24.5 %shard_map.64 = bf16[1024,128]{1,0:T(8,128)(2,1)S(1)} custom-call(bf16[8,128,128]{2,1,0:T(8,128)(2,1)} %bitcast.1, s32[8,5]{1,0:T(8,128)} %list_hbm.1, bf16[2,1024,640]{2,1,0:T(8,128)(2,1)} %near_hbm.1, bf16[2,1024,2048]{2,1,0:T(8,128)(2,1)} %col_hbm.1, bf16[2,1024,2048]{2,1,0:T(8,128)(2,1)} %mid_hbm.1, bf16[2,1024,1024]{2,1,0:T(8,128)(2,1)} %row_hbm.1), custom_call_target="tpu_custom_call" | custom-call | flops 3019898880 | bytes 23592960 | tf_op jit(solution)/shard_map/pallas_call | solution.py:267
  24.5 0.7 %copy.8 = bf16[1024,128]{1,0:T(8,128)(2,1)} copy(bf16[1024,128]{1,0:T(8,128)(2,1)S(1)} %shard_map.64) | data formatting | bytes 524288

commit v6 on v5

--- a/solution.py
+++ b/solution.py
@@ -206,6 +206,22 @@
                 copy.start()
                 b_copies.append(copy)
 
+    def landing(t):
+        for off_c in c_offs:
+            if y_offs[t] == 0 and off_c == 0:
+                continue
+            from_c = (core + nc - off_c) % nc
+            slot = landed.at[t, from_c]
+            pltpu.make_async_copy(slot, slot, b_recv.at[t, from_c]).wait()
+
+    def expand(t):
+        data = jnp.concatenate([landed[t, q] for q in range(nc)], axis=1)
+        return dot(data, row_t[t, 0]) + dot(swap(data), row_t[t, 1])
+
+    landing(ny - 1)
+    part = expand(ny - 1)
+    for i in range(leaves):
+        far[pl.ds(i * LEAF, LEAF), :] = part[:, i * LEAF : (i + 1) * LEAF].T
     for copy in halo:
         copy.wait_recv()
     load_near.wait()
@@ -222,24 +238,8 @@
             cols = pl.ds(j * LEAF, LEAF)
             part = dot(near[0, rows, cols], table[place]) + dot(near[1, rows, cols], turned[place])
             total = part if total is None else total + part
-        far[rows, :] = total
-
-    def landing(t):
-        for off_c in c_offs:
-            if y_offs[t] == 0 and off_c == 0:
-                continue
-            from_c = (core + nc - off_c) % nc
-            slot = landed.at[t, from_c]
-            pltpu.make_async_copy(slot, slot, b_recv.at[t, from_c]).wait()
-
-    def expand(t):
-        data = jnp.concatenate([landed[t, q] for q in range(nc)], axis=1)
-        return dot(data, row_t[t, 0]) + dot(swap(data), row_t[t, 1])
-
-    landing(ny - 1)
-    part = expand(ny - 1)
-    for i in range(leaves):
-        far[pl.ds(i * LEAF, LEAF), :] += part[:, i * LEAF : (i + 1) * LEAF].T
+        far[rows, :] += total
+
     for t in range(ny - 1):
         landing(t)
     part = sum(expand(t) for t in range(ny - 1))

time: 25.3 us -> 25.3 us (level)
  no operation moved by 1% of the time
where the time goes in v6:
time: 25.3 us; the launch traced here: 25.2 us
  Pallas kernels  24.5 us (97%)
  local copies, waits for them, and re-layouts  0.71 us (3%)
    pallas_call x1, Pallas kernels, on_device(): pl.pallas_call(functools.partial(kernel, nx, nz, ny, nc), out_shape=pltpu...  24.5 us
    unnamed x1, local copies, waits for them, and re-layouts  0.71 us

profile of v6, /device:TPU:1, one launch (start us, length us, event | category | flops | bytes accessed | tf_op | source)
XLA Modules:
  0.0 25.2 jit_solution(9839530284862416065)
XLA Ops:
  0.0 24.5 %shard_map.64 = bf16[1024,128]{1,0:T(8,128)(2,1)S(1)} custom-call(bf16[8,128,128]{2,1,0:T(8,128)(2,1)} %bitcast.1, s32[8,5]{1,0:T(8,128)} %list_hbm.1, bf16[2,1024,640]{2,1,0:T(8,128)(2,1)} %near_hbm.1, bf16[2,1024,2048]{2,1,0:T(8,128)(2,1)} %col_hbm.1, bf16[2,1024,2048]{2,1,0:T(8,128)(2,1)} %mid_hbm.1, bf16[2,1024,1024]{2,1,0:T(8,128)(2,1)} %row_hbm.1), custom_call_target="tpu_custom_call" | custom-call | flops 3019898880 | bytes 23592960 | tf_op jit(solution)/shard_map/pallas_call | solution.py:267
  24.5 0.7 %copy.8 = bf16[1024,128]{1,0:T(8,128)(2,1)} copy(bf16[1024,128]{1,0:T(8,128)(2,1)S(1)} %shard_map.64) | data formatting | bytes 524288
